TPU v7x, 256 devices: a whole 4x4x8 slice. The times are simulated.
256 devices in a mesh: tile: 64 (over z, y, core), lev: 4 (over x).
Axes of the slice: x: 4, y: 4, z: 8, core: 2. Of those that a mesh axis runs over, the one named last changes fastest.
Arguments:
- control: float32 [20, 1024, 4352], P('lev', 'tile'), may hold values from -6 to 6
- land_sea: int32 [1024, 4352], P('tile'), may hold values 0 or 1
- diffusivity: float32 [1024, 4352], P('tile'), may hold values from 0.22 to 0.245
- profile_counts: int32 [64], P('tile'), may hold values from 256 to 512, as said below
- owner_tile: int32 [32768, 1], P('tile'), may hold values from 0 to 63; in each aligned block of 512 rows (0 to 511, 512 to 1023, ...) at most 12 rows name the same one
- stencil_cells: int32 [32768, 4], P('tile'), may hold values from 0 to 69631
- stencil_weights: float32 [32768, 4], P('tile'), may hold values from 0.1 to 1
- inverse_error: float32 [32768, 20], P('tile', 'lev'), may hold values from 0.8 to 5
- correlation_inverse: float32 [20, 20], replicated, as said below
Outputs:
- product: float32 [20, 1024, 4352], P('lev', 'tile')
Inputs may be any that keep to these rules, and one draw needn't show every extreme that they name: `profile_counts`: every value lies between 256 and 512, and one block has all 512 slots live. `owner_tile`: among the 512 rows of one storage block no tile is named more than 12 times. `correlation_inverse`: symmetric.
All inputs are finite; a program needn't handle non-finite values. No bound on the sum of `land_sea` on one device may be relied on, other than what follows from the above.
Results may differ from a plain program's by a relative error of at most 0.00005.
Values sent between devices are 32-bit elements; how exact they have to be, the bound alone decides.
A program may use at most 128 MiB of HBM per device.

v0:
```python
import jax
import jax.numpy as jnp
from jax import lax
from jax.sharding import PartitionSpec as P

ITERS = 10


def padded(x, sides, width):
    for axis, dim in sides:
        size, length = (lax.axis_size(axis), x.shape[dim])
        up = [(i, (i + 1) % size) for i in range(size - 1)]
        down = [(j, i) for i, j in up]
        last = lax.slice_in_dim(x, length - width, length, axis=dim)
        initial = lax.slice_in_dim(x, 0, width, axis=dim)
        before = lax.ppermute(last, axis, up)
        after = lax.ppermute(initial, axis, down)
        x = jnp.concatenate([before, x, after], axis=dim)
    return x


def advance(values, edge_rows, edge_cols):
    flux_rows = edge_rows * (values[:, 1:] - values[:, :-1])
    flux_cols = edge_cols * (values[:, :, 1:] - values[:, :, :-1])
    flux_cols = jnp.pad(flux_cols, ((0, 0), (0, 0), (1, 1)))
    inner_cols = flux_cols[:, 1:-1]
    return (
        values[:, 1:-1]
        + (flux_rows[:, 1:] - flux_rows[:, :-1])
        + (inner_cols[:, :, 1:] - inner_cols[:, :, :-1])
    )


def run_block(extended, edge_rows, edge_cols):
    extended = advance(extended, edge_rows, edge_cols)
    return extended


def margin_depth():
    return 1


def diffuse(values, edge_rows, edge_cols):

    def single_sweep(counter, current):
        extended = padded(current, (("tile", 1),), 1)
        return run_block(extended, edge_rows, edge_cols)

    return lax.fori_loop(0, ITERS, single_sweep, values)


def per_device(
    control,
    land_sea,
    diffusivity,
    profile_counts,
    owner_tile,
    stencil_cells,
    stencil_weights,
    inverse_error,
    correlation_inverse,
):
    levels_here, height, columns = control.shape
    tile_count = lax.axis_size("tile")
    stored = owner_tile.shape[0]
    capacity = max(2, 3 * stored // (2 * tile_count))
    slot_total = tile_count * capacity
    reach_rows = margin_depth()
    ocean_mask = land_sea.astype(jnp.float32)
    half_edge = jnp.sqrt(ocean_mask * diffusivity)
    root_ext = padded(half_edge, (("tile", 0),), reach_rows)
    edge_rows = root_ext[1:] * root_ext[:-1]
    edge_cols = root_ext[:, 1:] * root_ext[:, :-1]
    background = diffuse(control * ocean_mask[None], edge_rows, edge_cols)
    owners = owner_tile[:, 0]
    living = jnp.arange(stored) < profile_counts[0]
    member = ((owners[:, None] == jnp.arange(tile_count)[None, :]) & living[:, None]).astype(
        jnp.int32
    )
    ranking = jnp.sum(jnp.cumsum(member, axis=0) * member, axis=1) - 1
    position = jnp.where(living, owners * capacity + ranking, slot_total)
    cell_buffer = jnp.zeros((slot_total, 4), jnp.int32).at[position].set(stencil_cells, mode="drop")
    payload = jnp.concatenate([stencil_weights, inverse_error], axis=1)
    payload_width = payload.shape[1]
    payload_buffer = (
        jnp.zeros((slot_total, payload_width), jnp.float32).at[position].set(payload, mode="drop")
    )
    cells_in = lax.all_to_all(
        cell_buffer.reshape(tile_count, capacity, 4),
        "tile",
        split_axis=0,
        concat_axis=0,
        tiled=True,
    ).reshape(slot_total * 4)
    payload_in = lax.all_to_all(
        payload_buffer.reshape(tile_count, capacity, payload_width),
        "tile",
        split_axis=0,
        concat_axis=0,
        tiled=True,
    ).reshape(slot_total, payload_width)
    weights_in = payload_in[:, :4]
    error_in = jnp.transpose(payload_in[:, 4:])
    picked = background.reshape(levels_here, height * columns)[:, cells_in].reshape(
        levels_here, slot_total, 4
    )
    modeled = jnp.sum(picked * weights_in[None], axis=2)
    scaled = modeled * error_in
    level_index = lax.axis_index("lev")
    own_rows = lax.dynamic_slice_in_dim(
        correlation_inverse, level_index * levels_here, levels_here, 0
    )
    gathered = lax.all_gather(scaled, "lev", axis=0, tiled=True)
    coupled = jnp.dot(
        own_rows, gathered, precision=lax.Precision.HIGHEST, preferred_element_type=jnp.float32
    )
    weighted = error_in * coupled
    spread = (weighted[:, :, None] * weights_in[None]).reshape(levels_here, slot_total * 4)
    adjoint = jnp.zeros((levels_here, height * columns), jnp.float32).at[:, cells_in].add(spread)
    returned = diffuse(adjoint.reshape(levels_here, height, columns), edge_rows, edge_cols)
    return control + returned * ocean_mask[None]


def solution(mesh):
    in_specs = (
        P("lev", "tile", None),
        P("tile", None),
        P("tile", None),
        P("tile"),
        P("tile", None),
        P("tile", None),
        P("tile", None),
        P("tile", "lev"),
        P(),
    )
    out_specs = P("lev", "tile", None)
    return jax.shard_map(
        per_device, mesh=mesh, in_specs=in_specs, out_specs=out_specs, check_vma=False
    )
```

profile of v0, /device:TPU:128, one launch (start us, length us, event | category | flops | bytes accessed | tf_op | source)
XLA Modules:
  0.0 425.7 jit_solution(2810110623888378559)
XLA Ops:
  8.1 10.5 %all-to-all-start = ((s32[64,12,4]{1,2,0:T(4,128)}), s32[64,12,4]{1,2,0:T(4,128)S(1)}, u32[]{:S(2)}, u32[]{:S(2)}) async-start(s32[64,12,4]{1,2,0:T(4,128)} %copy.28), calls=%async_computation | async-start | bytes 262144 | tf_op jit(solution)/shard_map/all_to_all | solution.py:88
  32.0 138.3 %while.24 = (s32[]{:T(128)}, f32[5,16,4352]{2,1,0:T(8,128)S(1)}, f32[17,4352]{1,0:T(8,128)S(1)}, f32[18,4351]{1,0:T(8,128)S(1)}, s32[]{:T(128)}) while((s32[]{:T(128)}, f32[5,16,4352]{2,1,0:T(8,128)S(1)}, f32[17,4352]{1,0:T(8,128)S(1)}, f32[18,4351]{1,0:T(8,128)S(1)}, s32[]{:T(128)}) %tuple.57), condition=%wide.region_6.7_spmd, body=%wide.region_5.6_spmd.sunk | while | flops 4438862 | bytes 19669668 | solution.py:49
  38.3 7.0 %collective-permute-done.1 = f32[5,1,4352]{2,1,0:T(1,128)S(1)} collective-permute-done((f32[5,1,4352]{2,1,0:T(1,128)S(1)}, f32[5,1,4352]{2,1,0:T(1,128)S(1)}, u32[]{:S(2)}, u32[]{:S(2)}) %collective-permute-start.1) | collective-permute-done | bytes 87072 | tf_op jit(solution)/shard_map/while/body/eval_jaxpr/ppermute | solution.py:16
  52.3 6.7 %collective-permute-done.1 = f32[5,1,4352]{2,1,0:T(1,128)S(1)} collective-permute-done((f32[5,1,4352]{2,1,0:T(1,128)S(1)}, f32[5,1,4352]{2,1,0:T(1,128)S(1)}, u32[]{:S(2)}, u32[]{:S(2)}) %collective-permute-start.1) | collective-permute-done | bytes 87072 | tf_op jit(solution)/shard_map/while/body/eval_jaxpr/ppermute | solution.py:16
  65.9 6.7 %collective-permute-done.1 = f32[5,1,4352]{2,1,0:T(1,128)S(1)} collective-permute-done((f32[5,1,4352]{2,1,0:T(1,128)S(1)}, f32[5,1,4352]{2,1,0:T(1,128)S(1)}, u32[]{:S(2)}, u32[]{:S(2)}) %collective-permute-start.1) | collective-permute-done | bytes 87072 | tf_op jit(solution)/shard_map/while/body/eval_jaxpr/ppermute | solution.py:16
  79.5 6.7 %collective-permute-done.1 = f32[5,1,4352]{2,1,0:T(1,128)S(1)} collective-permute-done((f32[5,1,4352]{2,1,0:T(1,128)S(1)}, f32[5,1,4352]{2,1,0:T(1,128)S(1)}, u32[]{:S(2)}, u32[]{:S(2)}) %collective-permute-start.1) | collective-permute-done | bytes 87072 | tf_op jit(solution)/shard_map/while/body/eval_jaxpr/ppermute | solution.py:16
  93.1 6.7 %collective-permute-done.1 = f32[5,1,4352]{2,1,0:T(1,128)S(1)} collective-permute-done((f32[5,1,4352]{2,1,0:T(1,128)S(1)}, f32[5,1,4352]{2,1,0:T(1,128)S(1)}, u32[]{:S(2)}, u32[]{:S(2)}) %collective-permute-start.1) | collective-permute-done | bytes 87072 | tf_op jit(solution)/shard_map/while/body/eval_jaxpr/ppermute | solution.py:16
  106.7 6.7 %collective-permute-done.1 = f32[5,1,4352]{2,1,0:T(1,128)S(1)} collective-permute-done((f32[5,1,4352]{2,1,0:T(1,128)S(1)}, f32[5,1,4352]{2,1,0:T(1,128)S(1)}, u32[]{:S(2)}, u32[]{:S(2)}) %collective-permute-start.1) | collective-permute-done | bytes 87072 | tf_op jit(solution)/shard_map/while/body/eval_jaxpr/ppermute | solution.py:16
  120.3 6.7 %collective-permute-done.1 = f32[5,1,4352]{2,1,0:T(1,128)S(1)} collective-permute-done((f32[5,1,4352]{2,1,0:T(1,128)S(1)}, f32[5,1,4352]{2,1,0:T(1,128)S(1)}, u32[]{:S(2)}, u32[]{:S(2)}) %collective-permute-start.1) | collective-permute-done | bytes 87072 | tf_op jit(solution)/shard_map/while/body/eval_jaxpr/ppermute | solution.py:16
  133.9 6.7 %collective-permute-done.1 = f32[5,1,4352]{2,1,0:T(1,128)S(1)} collective-permute-done((f32[5,1,4352]{2,1,0:T(1,128)S(1)}, f32[5,1,4352]{2,1,0:T(1,128)S(1)}, u32[]{:S(2)}, u32[]{:S(2)}) %collective-permute-start.1) | collective-permute-done | bytes 87072 | tf_op jit(solution)/shard_map/while/body/eval_jaxpr/ppermute | solution.py:16
  147.5 6.7 %collective-permute-done.1 = f32[5,1,4352]{2,1,0:T(1,128)S(1)} collective-permute-done((f32[5,1,4352]{2,1,0:T(1,128)S(1)}, f32[5,1,4352]{2,1,0:T(1,128)S(1)}, u32[]{:S(2)}, u32[]{:S(2)}) %collective-permute-start.1) | collective-permute-done | bytes 87072 | tf_op jit(solution)/shard_map/while/body/eval_jaxpr/ppermute | solution.py:16
  161.1 6.7 %collective-permute-done.1 = f32[5,1,4352]{2,1,0:T(1,128)S(1)} collective-permute-done((f32[5,1,4352]{2,1,0:T(1,128)S(1)}, f32[5,1,4352]{2,1,0:T(1,128)S(1)}, u32[]{:S(2)}, u32[]{:S(2)}) %collective-permute-start.1) | collective-permute-done | bytes 87072 | tf_op jit(solution)/shard_map/while/body/eval_jaxpr/ppermute | solution.py:16
  170.3 16.9 %copy.34 = f32[5,16,4352]{0,2,1:T(8,128)} copy(f32[5,16,4352]{2,1,0:T(8,128)S(1)} %get-tuple-element.111) | data formatting | bytes 2785280 | tf_op jit(solution)/shard_map/while | solution.py:49
  187.2 7.9 %all-to-all-start.1 = ((f32[64,12,9]{1,2,0:T(8,128)}), f32[64,12,9]{1,2,0:T(8,128)S(1)}, u32[]{:S(2)}, u32[]{:S(2)}) async-start(f32[64,12,9]{1,2,0:T(8,128)} %copy.32), calls=%async_computation.1 | async-start | bytes 1048576 | tf_op jit(solution)/shard_map/all_to_all | solution.py:95
  195.8 19.3 %gather_fusion = f32[3072,5]{1,0:T(8,128)S(1)} fusion(f32[5,69632]{0,1:T(8,128)} %bitcast.49, s32[3072]{0:T(1024)S(1)} %broadcast_clamp_fusion), kind=kCustom, calls=%fused_computation | custom fusion | bytes 135168 | tf_op jit(solution)/shard_map/gather | solution.py:104
  221.9 12.3 %all-gather = f32[4,5,768]{2,1,0:T(8,128)S(1)} all-gather(f32[1,5,768]{2,1,0:T(8,128)S(1)} %multiply_bitcast_fusion), channel_id=1, replica_groups=mesh['tile'=64,'lev'=4] {'lev'}, dimensions={0}, use_global_device_ids=true | all-gather | bytes 76800 | tf_op jit(solution)/shard_map/all_gather | solution.py:113
  234.8 32.7 %scatter_custom_fusion.2 = f32[5,69632]{0,1:T(8,128)} fusion(s32[3072]{0:T(1024)S(1)} %bitcast.53, f32[]{:T(128)} %constant.54.clone.1, f32[5,3072]{0,1:T(8,128)S(1)} %bitcast.50, f32[3072]{0:T(1024)S(1)} %mul.139), kind=kCustom, calls=%fused_computation.26 | custom fusion | flops 30720 | bytes 2977796 | tf_op jit(solution)/shard_map/scatter-add | solution.py:119
  267.5 19.4 %copy.39 = f32[5,16,4352]{2,1,0:T(8,128)S(1)} copy(f32[5,16,4352]{0,2,1:T(8,128)} %bitcast.48) | data formatting | bytes 2785280 | tf_op jit(solution)/shard_map/while | solution.py:49
  286.9 136.1 %while.25 = (s32[]{:T(128)}, f32[5,16,4352]{2,1,0:T(8,128)S(1)}, f32[17,4352]{1,0:T(8,128)S(1)}, f32[18,4351]{1,0:T(8,128)S(1)}, s32[]{:T(128)}) while((s32[]{:T(128)}, f32[5,16,4352]{2,1,0:T(8,128)S(1)}, f32[17,4352]{1,0:T(8,128)S(1)}, f32[18,4351]{1,0:T(8,128)S(1)}, s32[]{:T(128)}) %tuple.64), condition=%wide.region_10.11_spmd, body=%wide.region_9.10_spmd.sunk | while | flops 4438862 | bytes 19669668 | solution.py:49
  291.4 6.7 %collective-permute-done.3 = f32[5,1,4352]{2,1,0:T(1,128)S(1)} collective-permute-done((f32[5,1,4352]{2,1,0:T(1,128)S(1)}, f32[5,1,4352]{2,1,0:T(1,128)S(1)}, u32[]{:S(2)}, u32[]{:S(2)}) %collective-permute-start.3) | collective-permute-done | bytes 87072 | tf_op jit(solution)/shard_map/while/body/eval_jaxpr/ppermute | solution.py:16
  305.0 6.7 %collective-permute-done.3 = f32[5,1,4352]{2,1,0:T(1,128)S(1)} collective-permute-done((f32[5,1,4352]{2,1,0:T(1,128)S(1)}, f32[5,1,4352]{2,1,0:T(1,128)S(1)}, u32[]{:S(2)}, u32[]{:S(2)}) %collective-permute-start.3) | collective-permute-done | bytes 87072 | tf_op jit(solution)/shard_map/while/body/eval_jaxpr/ppermute | solution.py:16
  318.6 6.7 %collective-permute-done.3 = f32[5,1,4352]{2,1,0:T(1,128)S(1)} collective-permute-done((f32[5,1,4352]{2,1,0:T(1,128)S(1)}, f32[5,1,4352]{2,1,0:T(1,128)S(1)}, u32[]{:S(2)}, u32[]{:S(2)}) %collective-permute-start.3) | collective-permute-done | bytes 87072 | tf_op jit(solution)/shard_map/while/body/eval_jaxpr/ppermute | solution.py:16
  332.2 6.7 %collective-permute-done.3 = f32[5,1,4352]{2,1,0:T(1,128)S(1)} collective-permute-done((f32[5,1,4352]{2,1,0:T(1,128)S(1)}, f32[5,1,4352]{2,1,0:T(1,128)S(1)}, u32[]{:S(2)}, u32[]{:S(2)}) %collective-permute-start.3) | collective-permute-done | bytes 87072 | tf_op jit(solution)/shard_map/while/body/eval_jaxpr/ppermute | solution.py:16
  345.9 6.7 %collective-permute-done.3 = f32[5,1,4352]{2,1,0:T(1,128)S(1)} collective-permute-done((f32[5,1,4352]{2,1,0:T(1,128)S(1)}, f32[5,1,4352]{2,1,0:T(1,128)S(1)}, u32[]{:S(2)}, u32[]{:S(2)}) %collective-permute-start.3) | collective-permute-done | bytes 87072 | tf_op jit(solution)/shard_map/while/body/eval_jaxpr/ppermute | solution.py:16
  (230 shorter events, 203.5 us)
Async XLA Ops:
  8.1 179.0 %all-to-all-start = ((s32[64,12,4]{1,2,0:T(4,128)}), s32[64,12,4]{1,2,0:T(4,128)S(1)}, u32[]{:S(2)}, u32[]{:S(2)}) async-start(s32[64,12,4]{1,2,0:T(4,128)} %copy.28), calls=%async_computation | async-start | bytes 262144 | tf_op jit(solution)/shard_map/all_to_all | solution.py:88
  18.8 10.0 %collective-permute-start.4 = (f32[1,4352]{1,0:T(1,128)S(1)}, f32[1,4352]{1,0:T(1,128)S(1)}, u32[]{:S(2)}, u32[]{:S(2)}) collective-permute-start(f32[1,4352]{1,0:T(1,128)S(1)} %get-tuple-element.146), channel_id=1, source_target_pairs={{4,0},{8,4},{12,8},{16,12},{20,16},{24,20},{28,24},{32,28},{36,32}... | collective-permute-start | bytes 52232 | tf_op jit(solution)/shard_map/ppermute | solution.py:17
  23.3 8.4 %collective-permute-start.5 = (f32[1,4352]{1,0:T(1,128)S(1)}, f32[1,4352]{1,0:T(1,128)S(1)}, u32[]{:S(2)}, u32[]{:S(2)}) collective-permute-start(f32[1,4352]{1,0:T(1,128)S(1)} %get-tuple-element.145), channel_id=1, source_target_pairs={{0,4},{4,8},{8,12},{12,16},{16,20},{20,24},{24,28},{28,32},{32,36}... | collective-permute-start | bytes 52232 | tf_op jit(solution)/shard_map/ppermute | solution.py:16
  36.3 9.1 %collective-permute-start.1 = (f32[5,1,4352]{2,1,0:T(1,128)S(1)}, f32[5,1,4352]{2,1,0:T(1,128)S(1)}, u32[]{:S(2)}, u32[]{:S(2)}) collective-permute-start(f32[5,1,4352]{2,1,0:T(1,128)S(1)} %get-tuple-element.198), channel_id=1, source_target_pairs={{0,4},{4,8},{8,12},{12,16},{16,20},{20,24},{24,28},{28,32},{32,36}... | collective-permute-start | bytes 261128 | tf_op jit(solution)/shard_map/while/body/eval_jaxpr/ppermute | solution.py:16
  49.9 9.1 %collective-permute-start.1 = (f32[5,1,4352]{2,1,0:T(1,128)S(1)}, f32[5,1,4352]{2,1,0:T(1,128)S(1)}, u32[]{:S(2)}, u32[]{:S(2)}) collective-permute-start(f32[5,1,4352]{2,1,0:T(1,128)S(1)} %get-tuple-element.198), channel_id=1, source_target_pairs={{0,4},{4,8},{8,12},{12,16},{16,20},{20,24},{24,28},{28,32},{32,36}... | collective-permute-start | bytes 261128 | tf_op jit(solution)/shard_map/while/body/eval_jaxpr/ppermute | solution.py:16
  63.5 9.1 %collective-permute-start.1 = (f32[5,1,4352]{2,1,0:T(1,128)S(1)}, f32[5,1,4352]{2,1,0:T(1,128)S(1)}, u32[]{:S(2)}, u32[]{:S(2)}) collective-permute-start(f32[5,1,4352]{2,1,0:T(1,128)S(1)} %get-tuple-element.198), channel_id=1, source_target_pairs={{0,4},{4,8},{8,12},{12,16},{16,20},{20,24},{24,28},{28,32},{32,36}... | collective-permute-start | bytes 261128 | tf_op jit(solution)/shard_map/while/body/eval_jaxpr/ppermute | solution.py:16
  77.1 9.1 %collective-permute-start.1 = (f32[5,1,4352]{2,1,0:T(1,128)S(1)}, f32[5,1,4352]{2,1,0:T(1,128)S(1)}, u32[]{:S(2)}, u32[]{:S(2)}) collective-permute-start(f32[5,1,4352]{2,1,0:T(1,128)S(1)} %get-tuple-element.198), channel_id=1, source_target_pairs={{0,4},{4,8},{8,12},{12,16},{16,20},{20,24},{24,28},{28,32},{32,36}... | collective-permute-start | bytes 261128 | tf_op jit(solution)/shard_map/while/body/eval_jaxpr/ppermute | solution.py:16
  90.7 9.1 %collective-permute-start.1 = (f32[5,1,4352]{2,1,0:T(1,128)S(1)}, f32[5,1,4352]{2,1,0:T(1,128)S(1)}, u32[]{:S(2)}, u32[]{:S(2)}) collective-permute-start(f32[5,1,4352]{2,1,0:T(1,128)S(1)} %get-tuple-element.198), channel_id=1, source_target_pairs={{0,4},{4,8},{8,12},{12,16},{16,20},{20,24},{24,28},{28,32},{32,36}... | collective-permute-start | bytes 261128 | tf_op jit(solution)/shard_map/while/body/eval_jaxpr/ppermute | solution.py:16
  104.3 9.1 %collective-permute-start.1 = (f32[5,1,4352]{2,1,0:T(1,128)S(1)}, f32[5,1,4352]{2,1,0:T(1,128)S(1)}, u32[]{:S(2)}, u32[]{:S(2)}) collective-permute-start(f32[5,1,4352]{2,1,0:T(1,128)S(1)} %get-tuple-element.198), channel_id=1, source_target_pairs={{0,4},{4,8},{8,12},{12,16},{16,20},{20,24},{24,28},{28,32},{32,36}... | collective-permute-start | bytes 261128 | tf_op jit(solution)/shard_map/while/body/eval_jaxpr/ppermute | solution.py:16
  117.9 9.1 %collective-permute-start.1 = (f32[5,1,4352]{2,1,0:T(1,128)S(1)}, f32[5,1,4352]{2,1,0:T(1,128)S(1)}, u32[]{:S(2)}, u32[]{:S(2)}) collective-permute-start(f32[5,1,4352]{2,1,0:T(1,128)S(1)} %get-tuple-element.198), channel_id=1, source_target_pairs={{0,4},{4,8},{8,12},{12,16},{16,20},{20,24},{24,28},{28,32},{32,36}... | collective-permute-start | bytes 261128 | tf_op jit(solution)/shard_map/while/body/eval_jaxpr/ppermute | solution.py:16
  131.5 9.1 %collective-permute-start.1 = (f32[5,1,4352]{2,1,0:T(1,128)S(1)}, f32[5,1,4352]{2,1,0:T(1,128)S(1)}, u32[]{:S(2)}, u32[]{:S(2)}) collective-permute-start(f32[5,1,4352]{2,1,0:T(1,128)S(1)} %get-tuple-element.198), channel_id=1, source_target_pairs={{0,4},{4,8},{8,12},{12,16},{16,20},{20,24},{24,28},{28,32},{32,36}... | collective-permute-start | bytes 261128 | tf_op jit(solution)/shard_map/while/body/eval_jaxpr/ppermute | solution.py:16
  145.1 9.1 %collective-permute-start.1 = (f32[5,1,4352]{2,1,0:T(1,128)S(1)}, f32[5,1,4352]{2,1,0:T(1,128)S(1)}, u32[]{:S(2)}, u32[]{:S(2)}) collective-permute-start(f32[5,1,4352]{2,1,0:T(1,128)S(1)} %get-tuple-element.198), channel_id=1, source_target_pairs={{0,4},{4,8},{8,12},{12,16},{16,20},{20,24},{24,28},{28,32},{32,36}... | collective-permute-start | bytes 261128 | tf_op jit(solution)/shard_map/while/body/eval_jaxpr/ppermute | solution.py:16
  158.7 9.1 %collective-permute-start.1 = (f32[5,1,4352]{2,1,0:T(1,128)S(1)}, f32[5,1,4352]{2,1,0:T(1,128)S(1)}, u32[]{:S(2)}, u32[]{:S(2)}) collective-permute-start(f32[5,1,4352]{2,1,0:T(1,128)S(1)} %get-tuple-element.198), channel_id=1, source_target_pairs={{0,4},{4,8},{8,12},{12,16},{16,20},{20,24},{24,28},{28,32},{32,36}... | collective-permute-start | bytes 261128 | tf_op jit(solution)/shard_map/while/body/eval_jaxpr/ppermute | solution.py:16
  187.2 27.9 %all-to-all-start.1 = ((f32[64,12,9]{1,2,0:T(8,128)}), f32[64,12,9]{1,2,0:T(8,128)S(1)}, u32[]{:S(2)}, u32[]{:S(2)}) async-start(f32[64,12,9]{1,2,0:T(8,128)} %copy.32), calls=%async_computation.1 | async-start | bytes 1048576 | tf_op jit(solution)/shard_map/all_to_all | solution.py:95
  289.0 9.1 %collective-permute-start.3 = (f32[5,1,4352]{2,1,0:T(1,128)S(1)}, f32[5,1,4352]{2,1,0:T(1,128)S(1)}, u32[]{:S(2)}, u32[]{:S(2)}) collective-permute-start(f32[5,1,4352]{2,1,0:T(1,128)S(1)} %get-tuple-element.204), channel_id=1, source_target_pairs={{0,4},{4,8},{8,12},{12,16},{16,20},{20,24},{24,28},{28,32},{32,36}... | collective-permute-start | bytes 261128 | tf_op jit(solution)/shard_map/while/body/eval_jaxpr/ppermute | solution.py:16
  302.6 9.1 %collective-permute-start.3 = (f32[5,1,4352]{2,1,0:T(1,128)S(1)}, f32[5,1,4352]{2,1,0:T(1,128)S(1)}, u32[]{:S(2)}, u32[]{:S(2)}) collective-permute-start(f32[5,1,4352]{2,1,0:T(1,128)S(1)} %get-tuple-element.204), channel_id=1, source_target_pairs={{0,4},{4,8},{8,12},{12,16},{16,20},{20,24},{24,28},{28,32},{32,36}... | collective-permute-start | bytes 261128 | tf_op jit(solution)/shard_map/while/body/eval_jaxpr/ppermute | solution.py:16
  316.2 9.1 %collective-permute-start.3 = (f32[5,1,4352]{2,1,0:T(1,128)S(1)}, f32[5,1,4352]{2,1,0:T(1,128)S(1)}, u32[]{:S(2)}, u32[]{:S(2)}) collective-permute-start(f32[5,1,4352]{2,1,0:T(1,128)S(1)} %get-tuple-element.204), channel_id=1, source_target_pairs={{0,4},{4,8},{8,12},{12,16},{16,20},{20,24},{24,28},{28,32},{32,36}... | collective-permute-start | bytes 261128 | tf_op jit(solution)/shard_map/while/body/eval_jaxpr/ppermute | solution.py:16
  329.8 9.1 %collective-permute-start.3 = (f32[5,1,4352]{2,1,0:T(1,128)S(1)}, f32[5,1,4352]{2,1,0:T(1,128)S(1)}, u32[]{:S(2)}, u32[]{:S(2)}) collective-permute-start(f32[5,1,4352]{2,1,0:T(1,128)S(1)} %get-tuple-element.204), channel_id=1, source_target_pairs={{0,4},{4,8},{8,12},{12,16},{16,20},{20,24},{24,28},{28,32},{32,36}... | collective-permute-start | bytes 261128 | tf_op jit(solution)/shard_map/while/body/eval_jaxpr/ppermute | solution.py:16
  343.4 9.1 %collective-permute-start.3 = (f32[5,1,4352]{2,1,0:T(1,128)S(1)}, f32[5,1,4352]{2,1,0:T(1,128)S(1)}, u32[]{:S(2)}, u32[]{:S(2)}) collective-permute-start(f32[5,1,4352]{2,1,0:T(1,128)S(1)} %get-tuple-element.204), channel_id=1, source_target_pairs={{0,4},{4,8},{8,12},{12,16},{16,20},{20,24},{24,28},{28,32},{32,36}... | collective-permute-start | bytes 261128 | tf_op jit(solution)/shard_map/while/body/eval_jaxpr/ppermute | solution.py:16
  357.0 9.1 %collective-permute-start.3 = (f32[5,1,4352]{2,1,0:T(1,128)S(1)}, f32[5,1,4352]{2,1,0:T(1,128)S(1)}, u32[]{:S(2)}, u32[]{:S(2)}) collective-permute-start(f32[5,1,4352]{2,1,0:T(1,128)S(1)} %get-tuple-element.204), channel_id=1, source_target_pairs={{0,4},{4,8},{8,12},{12,16},{16,20},{20,24},{24,28},{28,32},{32,36}... | collective-permute-start | bytes 261128 | tf_op jit(solution)/shard_map/while/body/eval_jaxpr/ppermute | solution.py:16
  370.6 9.1 %collective-permute-start.3 = (f32[5,1,4352]{2,1,0:T(1,128)S(1)}, f32[5,1,4352]{2,1,0:T(1,128)S(1)}, u32[]{:S(2)}, u32[]{:S(2)}) collective-permute-start(f32[5,1,4352]{2,1,0:T(1,128)S(1)} %get-tuple-element.204), channel_id=1, source_target_pairs={{0,4},{4,8},{8,12},{12,16},{16,20},{20,24},{24,28},{28,32},{32,36}... | collective-permute-start | bytes 261128 | tf_op jit(solution)/shard_map/while/body/eval_jaxpr/ppermute | solution.py:16
  384.2 9.1 %collective-permute-start.3 = (f32[5,1,4352]{2,1,0:T(1,128)S(1)}, f32[5,1,4352]{2,1,0:T(1,128)S(1)}, u32[]{:S(2)}, u32[]{:S(2)}) collective-permute-start(f32[5,1,4352]{2,1,0:T(1,128)S(1)} %get-tuple-element.204), channel_id=1, source_target_pairs={{0,4},{4,8},{8,12},{12,16},{16,20},{20,24},{24,28},{28,32},{32,36}... | collective-permute-start | bytes 261128 | tf_op jit(solution)/shard_map/while/body/eval_jaxpr/ppermute | solution.py:16
  397.9 9.1 %collective-permute-start.3 = (f32[5,1,4352]{2,1,0:T(1,128)S(1)}, f32[5,1,4352]{2,1,0:T(1,128)S(1)}, u32[]{:S(2)}, u32[]{:S(2)}) collective-permute-start(f32[5,1,4352]{2,1,0:T(1,128)S(1)} %get-tuple-element.204), channel_id=1, source_target_pairs={{0,4},{4,8},{8,12},{12,16},{16,20},{20,24},{24,28},{28,32},{32,36}... | collective-permute-start | bytes 261128 | tf_op jit(solution)/shard_map/while/body/eval_jaxpr/ppermute | solution.py:16
  411.5 9.1 %collective-permute-start.3 = (f32[5,1,4352]{2,1,0:T(1,128)S(1)}, f32[5,1,4352]{2,1,0:T(1,128)S(1)}, u32[]{:S(2)}, u32[]{:S(2)}) collective-permute-start(f32[5,1,4352]{2,1,0:T(1,128)S(1)} %get-tuple-element.204), channel_id=1, source_target_pairs={{0,4},{4,8},{8,12},{12,16},{16,20},{20,24},{24,28},{28,32},{32,36}... | collective-permute-start | bytes 261128 | tf_op jit(solution)/shard_map/while/body/eval_jaxpr/ppermute | solution.py:16
  (27 other events, 382.9 us)
where the time goes:
time: 428 us; the launch traced here: 426 us
  waiting for transfers between devices  138 us (32%)
  starting transfers between devices  113 us (26%)
  other arithmetic  91.9 us (21%)
  local copies, waits for them, and re-layouts  68.4 us (16%)
  blocking collectives  12.3 us (3%)
    ppermute x21, waiting for transfers between devices, padded(): before = lax.ppermute(last, axis, up)  137 us
    ppermute x21, starting transfers between devices, padded(): before = lax.ppermute(last, axis, up)  49.6 us
    ppermute x21, starting transfers between devices, padded(): after = lax.ppermute(initial, axis, down)  45.1 us
    while x2, local copies, waits for them, and re-layouts, diffuse(): return lax.fori_loop(0, ITERS, single_sweep, values)  36.4 us
    scatter-add x1, other arithmetic, per_device(): jnp.zeros((levels_here, height * columns), jnp.float32).at[:, cells_in]  32.7 us
    add x20, other arithmetic, advance(): values[:, 1:-1] + (flux_rows[:, 1:] - flux_rows[:, :-1])  22.1 us
    gather x1, local copies, waits for them, and re-layouts, per_device(): background.reshape(levels_here, height * columns)[:, cells_in]  19.3 us
    mul x20, other arithmetic, advance(): flux_cols = edge_cols * (values[:, :, 1:] - values[:, :, :-1])  12.4 us
  transfers between devices with their start and end apart: 44, of which 22 were waited for; matrix products, arithmetic and copies ran while one was open for 15% of the time, Pallas kernels for 0%

commit v1 on v0

v1 whole, which is shorter than its diff:
```python
import functools

import jax
import jax.numpy as jnp
from jax import lax
from jax.experimental import pallas as pl
from jax.experimental.pallas import tpu as pltpu
from jax.sharding import PartitionSpec as P

ITERS = 10
DEPTH = ITERS
NEAR = 5
SRC = 64
RANKS = 12
F32, BF16 = jnp.float32, jnp.bfloat16
NT = (((1,), (1,)), ((), ()))


def up_to(n, m):
    return -(-n // m) * m


def kernel(dims, ctrl, land, diff, owner, cells, weights, errors, counts, corr, out,
           u, hb, ca, cb, rh, sbuf, rbuf, wk, ln, er, acc, oh, vf, vt, sv, xt, adj, sb,
           halo_send, halo_recv, prof_send, prof_recv, lev_send, lev_recv):
    tiles, levs, n_l, height, n_t, stored = dims
    pitch, body, front = n_t + 1, up_to((n_t + 1) * n_l, 8), 8
    hw = up_to(n_t, 8)
    qn, qp = height * n_t, up_to(height * n_t, 128)
    slots = RANKS * SRC
    tile, lev = lax.axis_index("tile"), lax.axis_index("lev")
    lane = lax.broadcasted_iota(jnp.int32, (1, 128), 1)
    first, last = lane == 0, lane == 127

    barrier = pltpu.get_barrier_semaphore()

    def greet(i, carry):
        pl.semaphore_signal(barrier, inc=1, device_id={"tile": lax.rem(tile + i, tiles)})
        return carry

    lax.fori_loop(1, tiles, greet, 0)
    for i in range(1, levs):
        pl.semaphore_signal(barrier, inc=1, device_id={"lev": lax.rem(lev + i, levs)})

    rows_all = height + 2 * DEPTH

    def clear(r, carry):
        for slot in range(4):
            u[slot, r, 0:front, :] = jnp.zeros((front, 128), F32)
            u[slot, r, front + body:front + body + 8, :] = jnp.zeros((8, 128), F32)
        hb[r, 0:8, :] = jnp.zeros((8, 128), F32)
        hb[r, 8 + hw:16 + hw, :] = jnp.zeros((8, 128), F32)
        return carry

    lax.fori_loop(0, rows_all, clear, 0)

    def clear_halo(lo):
        def one(r, carry):
            for slot in (0, 3):
                u[slot, r, front:front + body, :] = jnp.zeros((body, 128), F32)
            hb[r, 8:8 + hw, :] = jnp.zeros((hw, 128), F32)
            return carry

        lax.fori_loop(lo, lo + DEPTH, one, 0)

    @pl.when(tile == 0)
    def _():
        clear_halo(0)

    @pl.when(tile == tiles - 1)
    def _():
        clear_halo(DEPTH + height)

    for r in range(height):
        part, sub = r // 8, r % 8
        here = pl.ds(sub, n_t, stride=8)
        h = jnp.sqrt(land[part, here, :].astype(F32) * diff[part, here, :])
        hb[DEPTH + r, hw:8 + hw, :] = jnp.zeros((8, 128), F32)
        hb[DEPTH + r, 8:8 + n_t, :] = h
        rh[r, 0:n_t, :] = jnp.where(h > 0, 1.0 / h, 0.0)
        for l in range(n_l):
            at = front + pitch * l
            u[0, DEPTH + r, at:at + n_t, :] = h * ctrl[l, part, here, :]
            for slot in (0, 3):
                end = at + pitch if l < n_l - 1 else front + body
                u[slot, DEPTH + r, at + n_t:end, :] = jnp.zeros((end - at - n_t, 128), F32)

    spot = lax.broadcasted_iota(jnp.int32, (1, stored), 1)
    living = spot < counts[0]
    is_owner = jnp.where(
        (lax.broadcasted_iota(jnp.int32, (SRC, stored), 0) == owner[...]) & living, 1.0, 0.0
    )
    mine = is_owner.astype(BF16)
    before = jnp.where(
        lax.broadcasted_iota(jnp.int32, (stored, stored), 0)
        < lax.broadcasted_iota(jnp.int32, (stored, stored), 1), 1.0, 0.0
    ).astype(BF16)
    ahead = jnp.dot(mine, before, preferred_element_type=F32)
    rank = jnp.sum(ahead * is_owner, axis=0, keepdims=True)
    data = jnp.concatenate(
        [cells[...].astype(F32), weights[...], errors[...], jnp.zeros((8 - n_l, stored), F32)], axis=0
    )
    spread_out = jnp.concatenate([jnp.where(rank == float(r), data, 0.0) for r in range(16)], axis=0)
    message = jnp.zeros((SRC, 256), F32)
    left = spread_out
    for _ in range(3):
        piece = left.astype(BF16)
        message += lax.dot_general(mine, piece, NT, preferred_element_type=F32)
        left = left - piece.astype(F32)
    sbuf[...] = message.reshape(SRC, 1, 256)

    pl.semaphore_wait(barrier, tiles - 1 + levs - 1)

    def halo(which, side, chunk, root=False):
        lo, n = (0, NEAR) if chunk == 0 else (NEAR, DEPTH - NEAR)
        if side == 0:
            src, dst = DEPTH + lo, DEPTH + height + lo
        else:
            src, dst = height + DEPTH - lo - n, DEPTH - lo - n
        if root:
            a, b, which = hb.at[pl.ds(src, n), pl.ds(8, hw)], hb.at[pl.ds(dst, n), pl.ds(8, hw)], 2
        else:
            slot = 3 * which
            a = u.at[slot, pl.ds(src, n), pl.ds(front, body)]
            b = u.at[slot, pl.ds(dst, n), pl.ds(front, body)]
        return pltpu.make_async_remote_copy(
            src_ref=a, dst_ref=b, send_sem=halo_send.at[which, side, chunk], recv_sem=halo_recv.at[which, side, chunk],
            device_id={"tile": lax.rem(tile + (tiles - 1 if side == 0 else 1), tiles)},
        )

    def has(side):
        return tile > 0 if side == 0 else tile < tiles - 1

    def start_halo(which, chunk, root=False):
        for side in (0, 1):
            @pl.when(has(side))
            def _():
                halo(which, side, chunk, root).start()

    def wait_halo(which, chunk, root=False):
        for side in (0, 1):
            @pl.when(has(1 - side))
            def _():
                halo(which, side, chunk, root).wait_recv()

    def wait_sent(which, chunk, root=False):
        for side in (0, 1):
            @pl.when(has(side))
            def _():
                halo(which, side, chunk, root).wait_send()

    for chunk in (0, 1):
        start_halo(0, chunk, root=True)
        start_halo(0, chunk)

    def profile_copy(to, frm):
        return pltpu.make_async_remote_copy(
            src_ref=sbuf.at[to], dst_ref=rbuf.at[tile], send_sem=prof_send.at[to], recv_sem=prof_recv.at[frm],
            device_id={"tile": to},
        )

    def send_profiles(i, carry):
        to = lax.rem(tile + i, tiles)
        profile_copy(to, tile).start()
        return carry

    lax.fori_loop(1, tiles, send_profiles, 0)
    own = pltpu.make_async_copy(sbuf.at[tile], rbuf.at[tile], prof_recv.at[tile])
    own.start()

    def coefficients(lo, hi):
        def one(r, carry):
            h = hb[r, 8:8 + n_t, :]
            west = pltpu.roll(jnp.where(last, hb[r, 7:7 + n_t, :], h), 1, 1)
            east = pltpu.roll(jnp.where(first, hb[r, 9:9 + n_t, :], h), 127, 1)
            a = 1.0 - h * ((hb[r - 1, 8:8 + n_t, :] + hb[r + 1, 8:8 + n_t, :]) + (west + east))
            b = h * h
            for l in range(n_l):
                at = front + pitch * l
                end = at + pitch if l < n_l - 1 else front + body
                ca[r, at:at + n_t, :] = a
                cb[r, at:at + n_t, :] = b
                ca[r, at + n_t:end, :] = jnp.zeros((end - at - n_t, 128), F32)
                cb[r, at + n_t:end, :] = jnp.zeros((end - at - n_t, 128), F32)
            return carry

        lax.fori_loop(lo, hi, one, 0)

    def sweep(base, s, lo, hi):
        src, dst = jnp.where(s == 1, base, 1 + lax.rem(s, 2)), 1 + lax.rem(s + 1, 2)

        def one(r, carry):
            for j in range(front, front + body, 8):
                here = pl.ds(j, 8)
                c = u[src, r, here, :]
                west = pltpu.roll(jnp.where(last, u[src, r, j - 1:j + 7, :], c), 1, 1)
                east = pltpu.roll(jnp.where(first, u[src, r, j + 1:j + 9, :], c), 127, 1)
                around = (u[src, r - 1, here, :] + u[src, r + 1, here, :]) + (west + east)
                u[dst, r, here, :] = ca[r, here, :] * c + cb[r, here, :] * around
            return carry

        lax.fori_loop(lo + DEPTH, hi + DEPTH, one, 0)

    mid = height // 2

    def inner(base):
        def one(s, carry):
            sweep(base, s, s, height - s)
            return carry

        lax.fori_loop(1, mid, one, 0)

    def outer(base, old, new):
        def one(s, carry):
            sweep(base, s, s - new, jnp.minimum(s - old, mid))
            sweep(base, s, jnp.maximum(height - s + old, mid), height - s + new)
            return carry

        lax.fori_loop(1, ITERS + 1, one, 0)

    coefficients(DEPTH + 1, DEPTH + height - 1)
    inner(0)

    def got_profile(i, carry):
        frm = lax.rem(tile + i, tiles)
        profile_copy(frm, frm).wait_recv()
        return carry

    lax.fori_loop(1, tiles, got_profile, 0)
    own.wait()
    heard = jnp.concatenate([rbuf[...].reshape(SRC, 256), jnp.zeros((128 - SRC, 256), F32)], axis=0)
    turned = jnp.transpose(heard)
    for pair in range(RANKS // 2):
        both = turned[32 * pair:32 * pair + 16] + pltpu.roll(turned[32 * pair + 16:32 * pair + 32], SRC, 1)
        for k in range(4):
            where = pl.ds(k * slots + pair * 128, 128)
            cell = both[k:k + 1].astype(jnp.int32)
            wk[1:2, where] = (cell >> 7).astype(F32)
            ln[0:1, where] = cell & 127
            wk[0:1, where] = both[4 + k:5 + k]
        er[0:8, pl.ds(pair * 128, 128)] = both[8:16]

    def one_hots(i, carry):
        rows = lax.broadcasted_iota(jnp.int32, (128, 4 * slots), 0) + i * 128
        hot = jnp.where(rows == wk[1:2, :].astype(jnp.int32), 1.0, 0.0).astype(BF16)
        oh[pl.ds(pl.multiple_of(i * 128, 128), 128), :] = hot
        oh[pl.ds(pl.multiple_of(qp + i * 128, 128), 128), :] = hot
        return carry

    lax.fori_loop(0, qp // 128, one_hots, 0)

    wait_halo(0, 0, root=True)
    coefficients(DEPTH - NEAR + 1, DEPTH + 1)
    coefficients(DEPTH + height - 1, DEPTH + height + NEAR - 1)
    wait_halo(0, 0)
    outer(0, 0, NEAR)
    wait_halo(0, 1, root=True)
    coefficients(1, DEPTH - NEAR + 1)
    coefficients(DEPTH + height + NEAR - 1, rows_all - 1)
    wait_halo(0, 1)
    for chunk in (0, 1):
        wait_sent(0, chunk, root=True)
        wait_sent(0, chunk)
    outer(0, NEAR, DEPTH)

    for l in range(n_l):
        at = front + pitch * l
        for r in range(height):
            vf[l, r * n_t:(r + 1) * n_t, :] = rh[r, 0:n_t, :] * u[2, DEPTH + r, at:at + n_t, :]
        if qp > qn:
            vf[l, qn:qp, :] = jnp.zeros((qp - qn, 128), F32)

    def turn(l, carry):
        here = pl.ds(pl.multiple_of(l * 128, 128), 128)
        value = jnp.transpose(vf[l, :, :])
        high = value.astype(BF16)
        vt[here, 0:qp] = high
        vt[here, qp:2 * qp] = (value - high.astype(F32)).astype(BF16)
        return carry

    lax.fori_loop(0, n_l, turn, 0)
    acc[...] = jnp.zeros_like(acc)
    split = slots // 256

    def pick(i, carry):
        where = pl.ds(pl.multiple_of(i * 256, 256), 256)
        into = pl.ds(pl.multiple_of(lax.rem(i, split) * 256, 256), 256)
        got = jnp.dot(vt[...], oh[:, where], preferred_element_type=F32)
        on = lax.broadcasted_iota(jnp.int32, (128, 256), 0) == ln[0:1, where]
        weight = wk[0:1, where]
        for l in range(n_l):
            value = jnp.where(on, got[l * 128:(l + 1) * 128], 0.0).reshape(16, 8, 256)
            acc[l, :, into] += jnp.sum(value, axis=0) * weight
        return carry

    lax.fori_loop(0, 4 * split, pick, 0)
    sb[lev, :, :] = jnp.zeros((8, slots), F32)
    for l in range(n_l):
        sb[lev, l:l + 1, :] = jnp.sum(acc[l], axis=0, keepdims=True) * er[l:l + 1, :]

    def level_copy(i, back=False):
        other = lax.rem(lev + (levs - i if back else i), levs)
        return pltpu.make_async_remote_copy(
            src_ref=sb.at[lev], dst_ref=sb.at[other if back else lev], send_sem=lev_send.at[other],
            recv_sem=lev_recv.at[other if back else lev], device_id={"lev": other},
        )

    for i in range(1, levs):
        level_copy(i).start()
    for i in range(1, levs):
        level_copy(i, back=True).wait_recv()
    coupled = [jnp.zeros((1, slots), F32) for _ in range(n_l)]
    for m in range(levs):
        for j in range(n_l):
            row = sb[m, j:j + 1, :]
            for l in range(n_l):
                coupled[l] = coupled[l] + corr[n_l * lev + l, n_l * m + j] * row
    for l in range(n_l):
        weighted = coupled[l] * er[l:l + 1, :]
        for k in range(4):
            where = pl.ds(k * slots, slots)
            value = weighted * wk[0:1, where]
            high = value.astype(BF16).astype(F32)
            sv[l, 0:1, where] = high
            sv[n_l + l, 0:1, where] = value - high

    def put(i, carry):
        rows = lax.broadcasted_iota(jnp.int32, (128, 4 * slots), 0)
        on = rows == ln[0:1, :]
        for g in range(2):
            xt[g * 128:(g + 1) * 128, :] = jnp.where(on, sv[2 * i + g, 0:1, :], 0.0).astype(BF16)
        adj[i, 0:qn, :] = lax.dot_general(oh[0:qn, :], xt[...], NT, preferred_element_type=F32)
        return carry

    lax.fori_loop(0, n_l, put, 0)
    for r in range(height):
        h = hb[DEPTH + r, 8:8 + n_t, :]
        for l in range(n_l):
            at = front + pitch * l
            low = n_l + l
            both = (
                adj[l // 2, r * n_t:(r + 1) * n_t, (l % 2) * 128:(l % 2 + 1) * 128]
                + adj[low // 2, r * n_t:(r + 1) * n_t, (low % 2) * 128:(low % 2 + 1) * 128]
            )
            u[3, DEPTH + r, at:at + n_t, :] = h * both

    for chunk in (0, 1):
        start_halo(1, chunk)
    inner(3)
    wait_halo(1, 0)
    outer(3, 0, NEAR)
    wait_halo(1, 1)
    for chunk in (0, 1):
        wait_sent(1, chunk)
    outer(3, NEAR, DEPTH)

    for r in range(height):
        part, here = r // 8, pl.ds(r % 8, n_t, stride=8)
        for l in range(n_l):
            at = front + pitch * l
            out[l, part, here, :] = rh[r, 0:n_t, :] * u[2, DEPTH + r, at:at + n_t, :]

    def sent_profile(i, carry):
        profile_copy(lax.rem(tile + i, tiles), tile).wait_send()
        return carry

    lax.fori_loop(1, tiles, sent_profile, 0)
    for i in range(1, levs):
        level_copy(i).wait_send()


def tiled(x, height, n_t):
    lead = x.shape[:-2]
    n = len(lead)
    x = x.reshape(lead + (height // 8, 8, n_t, 128))
    x = jnp.swapaxes(x, n + 1, n + 2)
    return x.reshape(lead + (height // 8, n_t * 8, 128))


def untiled(x, height, n_t):
    lead = x.shape[:-3]
    n = len(lead)
    x = x.reshape(lead + (height // 8, n_t, 8, 128))
    x = jnp.swapaxes(x, n + 1, n + 2)
    return x.reshape(lead + (height, n_t * 128))


def per_device(dims, control, land_sea, diffusivity, profile_counts, owner_tile, stencil_cells, stencil_weights,
               inverse_error, correlation_inverse):
    tiles, levs, n_l, height, n_t, stored = dims
    body = up_to((n_t + 1) * n_l, 8)
    hw = up_to(n_t, 8)
    rows = height + 2 * DEPTH
    qn, qp = height * n_t, up_to(height * n_t, 128)
    slots = RANKS * SRC
    vmem = pl.BlockSpec(memory_space=pltpu.VMEM)
    smem = pl.BlockSpec(memory_space=pltpu.SMEM)
    returned = pl.pallas_call(
        functools.partial(kernel, dims),
        out_shape=jax.ShapeDtypeStruct((n_l, height // 8, n_t * 8, 128), F32),
        in_specs=[vmem] * 7 + [smem] * 2,
        out_specs=vmem,
        scratch_shapes=[
            pltpu.VMEM((4, rows, body + 16, 128), F32),
            pltpu.VMEM((rows, hw + 16, 128), F32),
            pltpu.VMEM((rows, body + 16, 128), F32),
            pltpu.VMEM((rows, body + 16, 128), F32),
            pltpu.VMEM((height, hw, 128), F32),
            pltpu.VMEM((SRC, 1, 256), F32),
            pltpu.VMEM((SRC, 1, 256), F32),
            pltpu.VMEM((2, 4 * slots), F32),
            pltpu.VMEM((1, 4 * slots), jnp.int32),
            pltpu.VMEM((8, slots), F32),
            pltpu.VMEM((n_l, 8, slots), F32),
            pltpu.VMEM((2 * qp, 4 * slots), BF16),
            pltpu.VMEM((n_l, qp, 128), F32),
            pltpu.VMEM((n_l * 128, 2 * qp), BF16),
            pltpu.VMEM((2 * n_l, 1, 4 * slots), F32),
            pltpu.VMEM((256, 4 * slots), BF16),
            pltpu.VMEM((n_l, up_to(qn, 8), 256), F32),
            pltpu.VMEM((levs, 8, slots), F32),
            pltpu.SemaphoreType.DMA((3, 2, 2)),
            pltpu.SemaphoreType.DMA((3, 2, 2)),
            pltpu.SemaphoreType.DMA((SRC,)),
            pltpu.SemaphoreType.DMA((SRC,)),
            pltpu.SemaphoreType.DMA((levs,)),
            pltpu.SemaphoreType.DMA((levs,)),
        ],
        compiler_params=pltpu.CompilerParams(
            collective_id=0, has_side_effects=True, vmem_limit_bytes=60 * 2**20
        ),
    )(
        tiled(control, height, n_t),
        tiled(land_sea, height, n_t),
        tiled(diffusivity, height, n_t),
        owner_tile.T,
        stencil_cells.T,
        stencil_weights.T,
        inverse_error.T,
        profile_counts,
        correlation_inverse,
    )
    return control + untiled(returned, height, n_t)


def solution(mesh):
    tiles, levs = mesh.shape["tile"], mesh.shape["lev"]

    def step(*args):
        n_l, height, columns = args[0].shape
        dims = (tiles, levs, n_l, height, columns // 128, args[4].shape[0])
        return per_device(dims, *args)

    return jax.shard_map(
        step,
        mesh=mesh,
        in_specs=(P("lev", "tile", None), P("tile", None), P("tile", None), P("tile"), P("tile", None), P("tile", None),
                  P("tile", None), P("tile", "lev"), P()),
        out_specs=P("lev", "tile", None),
        check_vma=False,
    )
```

time: 428 us -> 863 us (2.02)
  the two profiles are of different devices: /device:TPU:128 before, /device:TPU:1 now
where the time goes in v1:
time: 863 us
  Pallas kernels  860 us (100%)
    pallas_call x1, Pallas kernels, per_device(): pl.pallas_call(functools.partial(kernel, dims), out_shape=jax.ShapeDtypeS...  860 us

profile of v1, /device:TPU:1, one launch (start us, length us, event | category | flops | bytes accessed | tf_op | source)
XLA Modules:
  0.0 863.2 jit_solution(16770463335715791671)
XLA Ops:
  0.7 0.0 copy-start
  0.7 860.0 %shard_map.91 = f32[5,2,272,128]{3,2,1,0:T(8,128)} custom-call(f32[5,2,272,128]{3,2,1,0:T(8,128)} %bitcast.25, s32[2,272,128]{2,1,0:T(8,128)} %bitcast.26, f32[2,272,128]{2,1,0:T(8,128)} %bitcast.27, s32[1,512]{1,0:T(1,128)} %bitcast.31, s32[4,512]{1,0:T(4,128)} %bitcast.29, f32[4,512]{1,0:T(4,128)} %bitcast.30, f32[5,512]{1,0:T(8,128)} %bitcast.28, ...), custom_call_target="tpu_custom_call" | custom-call | tf_op jit(solution)/shard_map/pallas_call | solution.py:398
  860.6 0.0 copy-done
  860.6 2.6 bitcast_add_fusion
Async XLA Ops:
  0.7 860.0 %copy-start = (f32[5,16,4352]{2,1,0:T(8,128)S(1)}, f32[5,16,4352]{2,1,0:T(8,128)}, u32[]{:S(2)}) copy-start(f32[5,16,4352]{2,1,0:T(8,128)} %param.9) | copy-start | bytes 4177924

commit v2 on v1

--- a/solution.py
+++ b/solution.py
@@ -21,7 +21,7 @@
 
 
 def kernel(dims, ctrl, land, diff, owner, cells, weights, errors, counts, corr, out,
-           u, hb, ca, cb, rh, sbuf, rbuf, wk, ln, er, acc, oh, vf, vt, sv, xt, adj, sb,
+           u0, u1, u2, u3, hb, ca, cb, rh, sbuf, rbuf, wk, ln, er, acc, oh, vf, vt, sv, xt, adj, sb,
            halo_send, halo_recv, prof_send, prof_recv, lev_send, lev_recv):
     tiles, levs, n_l, height, n_t, stored = dims
     pitch, body, front = n_t + 1, up_to((n_t + 1) * n_l, 8), 8
@@ -45,9 +45,9 @@
     rows_all = height + 2 * DEPTH
 
     def clear(r, carry):
-        for slot in range(4):
-            u[slot, r, 0:front, :] = jnp.zeros((front, 128), F32)
-            u[slot, r, front + body:front + body + 8, :] = jnp.zeros((8, 128), F32)
+        for u in (u0, u1, u2, u3):
+            u[r, 0:front, :] = jnp.zeros((front, 128), F32)
+            u[r, front + body:front + body + 8, :] = jnp.zeros((8, 128), F32)
         hb[r, 0:8, :] = jnp.zeros((8, 128), F32)
         hb[r, 8 + hw:16 + hw, :] = jnp.zeros((8, 128), F32)
         return carry
@@ -56,8 +56,8 @@
 
     def clear_halo(lo):
         def one(r, carry):
-            for slot in (0, 3):
-                u[slot, r, front:front + body, :] = jnp.zeros((body, 128), F32)
+            for u in (u0, u3):
+                u[r, front:front + body, :] = jnp.zeros((body, 128), F32)
             hb[r, 8:8 + hw, :] = jnp.zeros((hw, 128), F32)
             return carry
 
@@ -80,10 +80,10 @@
         rh[r, 0:n_t, :] = jnp.where(h > 0, 1.0 / h, 0.0)
         for l in range(n_l):
             at = front + pitch * l
-            u[0, DEPTH + r, at:at + n_t, :] = h * ctrl[l, part, here, :]
-            for slot in (0, 3):
+            u0[DEPTH + r, at:at + n_t, :] = h * ctrl[l, part, here, :]
+            for u in (u0, u3):
                 end = at + pitch if l < n_l - 1 else front + body
-                u[slot, DEPTH + r, at + n_t:end, :] = jnp.zeros((end - at - n_t, 128), F32)
+                u[DEPTH + r, at + n_t:end, :] = jnp.zeros((end - at - n_t, 128), F32)
 
     spot = lax.broadcasted_iota(jnp.int32, (1, stored), 1)
     living = spot < counts[0]
@@ -120,9 +120,8 @@
         if root:
             a, b, which = hb.at[pl.ds(src, n), pl.ds(8, hw)], hb.at[pl.ds(dst, n), pl.ds(8, hw)], 2
         else:
-            slot = 3 * which
-            a = u.at[slot, pl.ds(src, n), pl.ds(front, body)]
-            b = u.at[slot, pl.ds(dst, n), pl.ds(front, body)]
+            u = (u0, u3)[which]
+            a, b = u.at[pl.ds(src, n), pl.ds(front, body)], u.at[pl.ds(dst, n), pl.ds(front, body)]
         return pltpu.make_async_remote_copy(
             src_ref=a, dst_ref=b, send_sem=halo_send.at[which, side, chunk], recv_sem=halo_recv.at[which, side, chunk],
             device_id={"tile": lax.rem(tile + (tiles - 1 if side == 0 else 1), tiles)},
@@ -186,40 +185,45 @@
 
         lax.fori_loop(lo, hi, one, 0)
 
-    def sweep(base, s, lo, hi):
-        src, dst = jnp.where(s == 1, base, 1 + lax.rem(s, 2)), 1 + lax.rem(s + 1, 2)
-
-        def one(r, carry):
-            for j in range(front, front + body, 8):
-                here = pl.ds(j, 8)
-                c = u[src, r, here, :]
-                west = pltpu.roll(jnp.where(last, u[src, r, j - 1:j + 7, :], c), 1, 1)
-                east = pltpu.roll(jnp.where(first, u[src, r, j + 1:j + 9, :], c), 127, 1)
-                around = (u[src, r - 1, here, :] + u[src, r + 1, here, :]) + (west + east)
-                u[dst, r, here, :] = ca[r, here, :] * c + cb[r, here, :] * around
+    mid = height // 2
+
+    def sweep(src, dst, lo, n):
+        def one(i, carry):
+            for r in (DEPTH + lo + i, DEPTH + height - 1 - lo - i):
+                made = []
+                for j in range(front, front + body, 8):
+                    here = pl.ds(j, 8)
+                    c = src[r, here, :]
+                    west = pltpu.roll(jnp.where(last, src[r, j - 1:j + 7, :], c), 1, 1)
+                    east = pltpu.roll(jnp.where(first, src[r, j + 1:j + 9, :], c), 127, 1)
+                    around = (src[r - 1, here, :] + src[r + 1, here, :]) + (west + east)
+                    made.append(ca[r, here, :] * c + cb[r, here, :] * around)
+                for j, value in zip(range(front, front + body, 8), made):
+                    dst[r, pl.ds(j, 8), :] = value
             return carry
 
-        lax.fori_loop(lo + DEPTH, hi + DEPTH, one, 0)
-
-    mid = height // 2
-
-    def inner(base):
-        def one(s, carry):
-            sweep(base, s, s, height - s)
+        lax.fori_loop(0, n, one, 0)
+
+    def steps(begin, reach, total):
+        sweep(begin, u1, *reach(1))
+
+        def two(t, carry):
+            sweep(u1, u2, *reach(2 * t))
+            sweep(u2, u1, *reach(2 * t + 1))
             return carry
 
-        lax.fori_loop(1, mid, one, 0)
-
-    def outer(base, old, new):
-        def one(s, carry):
-            sweep(base, s, s - new, jnp.minimum(s - old, mid))
-            sweep(base, s, jnp.maximum(height - s + old, mid), height - s + new)
-            return carry
-
-        lax.fori_loop(1, ITERS + 1, one, 0)
+        lax.fori_loop(1, (total + 1) // 2, two, 0)
+        if total % 2 == 0:
+            sweep(u1, u2, *reach(total))
+
+    def inner(begin):
+        steps(begin, lambda s: (s, mid - s), mid - 1)
+
+    def outer(begin, old, new):
+        steps(begin, lambda s: (s - new, jnp.minimum(new - old, mid + new - s)), ITERS)
 
     coefficients(DEPTH + 1, DEPTH + height - 1)
-    inner(0)
+    inner(u0)
 
     def got_profile(i, carry):
         frm = lax.rem(tile + i, tiles)
@@ -253,7 +257,7 @@
     coefficients(DEPTH - NEAR + 1, DEPTH + 1)
     coefficients(DEPTH + height - 1, DEPTH + height + NEAR - 1)
     wait_halo(0, 0)
-    outer(0, 0, NEAR)
+    outer(u0, 0, NEAR)
     wait_halo(0, 1, root=True)
     coefficients(1, DEPTH - NEAR + 1)
     coefficients(DEPTH + height + NEAR - 1, rows_all - 1)
@@ -261,12 +265,12 @@
     for chunk in (0, 1):
         wait_sent(0, chunk, root=True)
         wait_sent(0, chunk)
-    outer(0, NEAR, DEPTH)
+    outer(u0, NEAR, DEPTH)
 
     for l in range(n_l):
         at = front + pitch * l
         for r in range(height):
-            vf[l, r * n_t:(r + 1) * n_t, :] = rh[r, 0:n_t, :] * u[2, DEPTH + r, at:at + n_t, :]
+            vf[l, r * n_t:(r + 1) * n_t, :] = rh[r, 0:n_t, :] * u2[DEPTH + r, at:at + n_t, :]
         if qp > qn:
             vf[l, qn:qp, :] = jnp.zeros((qp - qn, 128), F32)
 
@@ -342,23 +346,23 @@
                 adj[l // 2, r * n_t:(r + 1) * n_t, (l % 2) * 128:(l % 2 + 1) * 128]
                 + adj[low // 2, r * n_t:(r + 1) * n_t, (low % 2) * 128:(low % 2 + 1) * 128]
             )
-            u[3, DEPTH + r, at:at + n_t, :] = h * both
+            u3[DEPTH + r, at:at + n_t, :] = h * both
 
     for chunk in (0, 1):
         start_halo(1, chunk)
-    inner(3)
+    inner(u3)
     wait_halo(1, 0)
-    outer(3, 0, NEAR)
+    outer(u3, 0, NEAR)
     wait_halo(1, 1)
     for chunk in (0, 1):
         wait_sent(1, chunk)
-    outer(3, NEAR, DEPTH)
+    outer(u3, NEAR, DEPTH)
 
     for r in range(height):
         part, here = r // 8, pl.ds(r % 8, n_t, stride=8)
         for l in range(n_l):
             at = front + pitch * l
-            out[l, part, here, :] = rh[r, 0:n_t, :] * u[2, DEPTH + r, at:at + n_t, :]
+            out[l, part, here, :] = rh[r, 0:n_t, :] * u2[DEPTH + r, at:at + n_t, :]
 
     def sent_profile(i, carry):
         profile_copy(lax.rem(tile + i, tiles), tile).wait_send()
@@ -401,7 +405,7 @@
         in_specs=[vmem] * 7 + [smem] * 2,
         out_specs=vmem,
         scratch_shapes=[
-            pltpu.VMEM((4, rows, body + 16, 128), F32),
+            *[pltpu.VMEM((rows, body + 16, 128), F32) for _ in range(4)],
             pltpu.VMEM((rows, hw + 16, 128), F32),
             pltpu.VMEM((rows, body + 16, 128), F32),
             pltpu.VMEM((rows, body + 16, 128), F32),

time: 863 us -> 98.5 us (0.11)
  Pallas kernels: 860 us -> 95.1 us
    pallas_call x1, Pallas kernels: 860 us -> 95.1 us  [per_device(): pl.pallas_call(functools.partial(kernel, dims), out_shape=jax.ShapeDtypeS...]
where the time goes in v2:
time: 98.5 us; the launch traced here: 98.3 us
  Pallas kernels  95.1 us (97%)
  other arithmetic  2.57 us (3%)
    pallas_call x1, Pallas kernels, per_device(): pl.pallas_call(functools.partial(kernel, dims), out_shape=jax.ShapeDtypeS...  95.1 us
    add x1, other arithmetic, per_device(): return control + untiled(returned, height, n_t)  2.57 us

profile of v2, /device:TPU:1, one launch (start us, length us, event | category | flops | bytes accessed | tf_op | source)
XLA Modules:
  0.0 98.3 jit_solution(16544595281336130356)
XLA Ops:
  0.7 0.0 copy-start
  0.7 95.1 %shard_map.91 = f32[5,2,272,128]{3,2,1,0:T(8,128)} custom-call(f32[5,2,272,128]{3,2,1,0:T(8,128)} %bitcast.25, s32[2,272,128]{2,1,0:T(8,128)} %bitcast.26, f32[2,272,128]{2,1,0:T(8,128)} %bitcast.27, s32[1,512]{1,0:T(1,128)} %bitcast.31, s32[4,512]{1,0:T(4,128)} %bitcast.29, f32[4,512]{1,0:T(4,128)} %bitcast.30, f32[5,512]{1,0:T(8,128)} %bitcast.28, ...), custom_call_target="tpu_custom_call" | custom-call | tf_op jit(solution)/shard_map/pallas_call | solution.py:402
  95.8 0.0 copy-done
  95.8 2.6 %bitcast_add_fusion = f32[5,16,4352]{2,1,0:T(8,128)} fusion(f32[5,16,4352]{2,1,0:T(8,128)S(1)} %copy-done, f32[5,2,272,128]{3,2,1,0:T(8,128)} %shard_map.91), kind=kLoop, calls=%fused_computation | loop fusion | flops 348160 | bytes 4177920 | tf_op jit(solution)/shard_map/add | solution.py:447
Async XLA Ops:
  0.7 95.1 %copy-start = (f32[5,16,4352]{2,1,0:T(8,128)S(1)}, f32[5,16,4352]{2,1,0:T(8,128)}, u32[]{:S(2)}) copy-start(f32[5,16,4352]{2,1,0:T(8,128)} %param.9) | copy-start | bytes 4177924

commit v3 on v2

--- a/solution.py
+++ b/solution.py
@@ -9,7 +9,7 @@
 
 ITERS = 10
 DEPTH = ITERS
-NEAR = 5
+CHUNK = 2
 SRC = 64
 RANKS = 12
 F32, BF16 = jnp.float32, jnp.bfloat16
@@ -84,6 +84,55 @@
             for u in (u0, u3):
                 end = at + pitch if l < n_l - 1 else front + body
                 u[DEPTH + r, at + n_t:end, :] = jnp.zeros((end - at - n_t, 128), F32)
+
+    pl.semaphore_wait(barrier, tiles - 1 + levs - 1)
+
+    def halo(which, side, chunk, root=False):
+        lo, n = chunk * CHUNK, CHUNK
+        if side == 0:
+            src, dst = DEPTH + lo, DEPTH + height + lo
+        else:
+            src, dst = height + DEPTH - lo - n, DEPTH - lo - n
+        if root:
+            a, b, which = hb.at[pl.ds(src, n), pl.ds(8, hw)], hb.at[pl.ds(dst, n), pl.ds(8, hw)], 2
+        else:
+            u = (u0, u3)[which]
+            a, b = u.at[pl.ds(src, n), pl.ds(front, body)], u.at[pl.ds(dst, n), pl.ds(front, body)]
+        return pltpu.make_async_remote_copy(
+            src_ref=a, dst_ref=b, send_sem=halo_send.at[which, side, chunk], recv_sem=halo_recv.at[which, side, chunk],
+            device_id={"tile": lax.rem(tile + (tiles - 1 if side == 0 else 1), tiles)},
+        )
+
+    def has(side):
+        return tile > 0 if side == 0 else tile < tiles - 1
+
+    def start_halo(which, chunk, root=False):
+        for side in (0, 1):
+            @pl.when(has(side))
+            def _():
+                halo(which, side, chunk, root).start()
+
+    def wait_halo(which, chunk, root=False):
+        for side in (0, 1):
+            @pl.when(has(1 - side))
+            def _():
+                halo(which, side, chunk, root).wait_recv()
+
+    def wait_sent(which, chunk, root=False):
+        for side in (0, 1):
+            @pl.when(has(side))
+            def _():
+                halo(which, side, chunk, root).wait_send()
+
+    chunks = DEPTH // CHUNK
+
+    def start_first(chunk, carry):
+        start_halo(0, chunk, root=True)
+        start_halo(0, chunk)
+        return carry
+
+    lax.fori_loop(0, chunks, start_first, 0)
+
 
     spot = lax.broadcasted_iota(jnp.int32, (1, stored), 1)
     living = spot < counts[0]
@@ -109,49 +158,6 @@
         left = left - piece.astype(F32)
     sbuf[...] = message.reshape(SRC, 1, 256)
 
-    pl.semaphore_wait(barrier, tiles - 1 + levs - 1)
-
-    def halo(which, side, chunk, root=False):
-        lo, n = (0, NEAR) if chunk == 0 else (NEAR, DEPTH - NEAR)
-        if side == 0:
-            src, dst = DEPTH + lo, DEPTH + height + lo
-        else:
-            src, dst = height + DEPTH - lo - n, DEPTH - lo - n
-        if root:
-            a, b, which = hb.at[pl.ds(src, n), pl.ds(8, hw)], hb.at[pl.ds(dst, n), pl.ds(8, hw)], 2
-        else:
-            u = (u0, u3)[which]
-            a, b = u.at[pl.ds(src, n), pl.ds(front, body)], u.at[pl.ds(dst, n), pl.ds(front, body)]
-        return pltpu.make_async_remote_copy(
-            src_ref=a, dst_ref=b, send_sem=halo_send.at[which, side, chunk], recv_sem=halo_recv.at[which, side, chunk],
-            device_id={"tile": lax.rem(tile + (tiles - 1 if side == 0 else 1), tiles)},
-        )
-
-    def has(side):
-        return tile > 0 if side == 0 else tile < tiles - 1
-
-    def start_halo(which, chunk, root=False):
-        for side in (0, 1):
-            @pl.when(has(side))
-            def _():
-                halo(which, side, chunk, root).start()
-
-    def wait_halo(which, chunk, root=False):
-        for side in (0, 1):
-            @pl.when(has(1 - side))
-            def _():
-                halo(which, side, chunk, root).wait_recv()
-
-    def wait_sent(which, chunk, root=False):
-        for side in (0, 1):
-            @pl.when(has(side))
-            def _():
-                halo(which, side, chunk, root).wait_send()
-
-    for chunk in (0, 1):
-        start_halo(0, chunk, root=True)
-        start_halo(0, chunk)
-
     def profile_copy(to, frm):
         return pltpu.make_async_remote_copy(
             src_ref=sbuf.at[to], dst_ref=rbuf.at[tile], send_sem=prof_send.at[to], recv_sem=prof_recv.at[frm],
@@ -219,8 +225,36 @@
     def inner(begin):
         steps(begin, lambda s: (s, mid - s), mid - 1)
 
-    def outer(begin, old, new):
-        steps(begin, lambda s: (s - new, jnp.minimum(new - old, mid + new - s)), ITERS)
+    def nearest(begin):
+        steps(begin, lambda s: (s - CHUNK, jnp.minimum(CHUNK, mid + CHUNK - s)), ITERS)
+
+    def both_ends(src, dst, lo):
+        for top in (DEPTH + lo, DEPTH + height - lo - CHUNK):
+            for half in range(front, front + body, body // 2):
+                made = []
+                for j in range(half, half + body // 2, 8):
+                    here = pl.ds(j, 8)
+                    c = [src[top + i, here, :] for i in range(-1, CHUNK + 1)]
+                    for i in range(CHUNK):
+                        r, own = top + i, c[i + 1]
+                        west = pltpu.roll(jnp.where(last, src[r, j - 1:j + 7, :], own), 1, 1)
+                        east = pltpu.roll(jnp.where(first, src[r, j + 1:j + 9, :], own), 127, 1)
+                        around = (c[i] + c[i + 2]) + (west + east)
+                        made.append((r, here, ca[r, here, :] * own + cb[r, here, :] * around))
+                for r, here, value in made:
+                    dst[r, here, :] = value
+
+    def farther(begin, chunk):
+        lo = -CHUNK * (chunk + 1)
+        both_ends(begin, u1, lo + 1)
+
+        def two(t, carry):
+            both_ends(u1, u2, lo + 2 * t)
+            both_ends(u2, u1, lo + 2 * t + 1)
+            return carry
+
+        lax.fori_loop(1, ITERS // 2, two, 0)
+        both_ends(u1, u2, lo + ITERS)
 
     coefficients(DEPTH + 1, DEPTH + height - 1)
     inner(u0)
@@ -253,19 +287,28 @@
 
     lax.fori_loop(0, qp // 128, one_hots, 0)
 
-    wait_halo(0, 0, root=True)
-    coefficients(DEPTH - NEAR + 1, DEPTH + 1)
-    coefficients(DEPTH + height - 1, DEPTH + height + NEAR - 1)
-    wait_halo(0, 0)
-    outer(u0, 0, NEAR)
-    wait_halo(0, 1, root=True)
-    coefficients(1, DEPTH - NEAR + 1)
-    coefficients(DEPTH + height + NEAR - 1, rows_all - 1)
-    wait_halo(0, 1)
-    for chunk in (0, 1):
+    def more_roots(chunk):
+        wait_halo(0, chunk, root=True)
+        coefficients(DEPTH - CHUNK * chunk - 1, DEPTH - CHUNK * chunk + 1)
+        coefficients(DEPTH + height + CHUNK * chunk - 1, DEPTH + height + CHUNK * chunk + 1)
+        wait_halo(0, chunk)
+
+    more_roots(0)
+    nearest(u0)
+
+    def arrived(chunk, carry):
+        more_roots(chunk)
+        farther(u0, chunk)
+        return carry
+
+    lax.fori_loop(1, chunks, arrived, 0)
+
+    def all_sent(chunk, carry):
         wait_sent(0, chunk, root=True)
         wait_sent(0, chunk)
-    outer(u0, NEAR, DEPTH)
+        return carry
+
+    lax.fori_loop(0, chunks, all_sent, 0)
 
     for l in range(n_l):
         at = front + pitch * l
@@ -348,15 +391,27 @@
             )
             u3[DEPTH + r, at:at + n_t, :] = h * both
 
-    for chunk in (0, 1):
+    def start_second(chunk, carry):
         start_halo(1, chunk)
+        return carry
+
+    lax.fori_loop(0, chunks, start_second, 0)
     inner(u3)
     wait_halo(1, 0)
-    outer(u3, 0, NEAR)
-    wait_halo(1, 1)
-    for chunk in (0, 1):
+    nearest(u3)
+
+    def arrived_again(chunk, carry):
+        wait_halo(1, chunk)
+        farther(u3, chunk)
+        return carry
+
+    lax.fori_loop(1, chunks, arrived_again, 0)
+
+    def all_sent_again(chunk, carry):
         wait_sent(1, chunk)
-    outer(u3, NEAR, DEPTH)
+        return carry
+
+    lax.fori_loop(0, chunks, all_sent_again, 0)
 
     for r in range(height):
         part, here = r // 8, pl.ds(r % 8, n_t, stride=8)
@@ -423,8 +478,8 @@
             pltpu.VMEM((256, 4 * slots), BF16),
             pltpu.VMEM((n_l, up_to(qn, 8), 256), F32),
             pltpu.VMEM((levs, 8, slots), F32),
-            pltpu.SemaphoreType.DMA((3, 2, 2)),
-            pltpu.SemaphoreType.DMA((3, 2, 2)),
+            pltpu.SemaphoreType.DMA((3, 2, DEPTH // CHUNK)),
+            pltpu.SemaphoreType.DMA((3, 2, DEPTH // CHUNK)),
             pltpu.SemaphoreType.DMA((SRC,)),
             pltpu.SemaphoreType.DMA((SRC,)),
             pltpu.SemaphoreType.DMA((levs,)),

time: 98.5 us -> 90.4 us (0.918)
  Pallas kernels: 95.1 us -> 87 us
    pallas_call x1, Pallas kernels: 95.1 us -> 87 us  [per_device(): pl.pallas_call(functools.partial(kernel, dims), out_shape=jax.ShapeDtypeS...]
where the time goes in v3:
time: 90.4 us; the launch traced here: 90.2 us
  Pallas kernels  87 us (96%)
  other arithmetic  2.57 us (3%)
    pallas_call x1, Pallas kernels, per_device(): pl.pallas_call(functools.partial(kernel, dims), out_shape=jax.ShapeDtypeS...  87 us
    add x1, other arithmetic, per_device(): return control + untiled(returned, height, n_t)  2.57 us

profile of v3, /device:TPU:1, one launch (start us, length us, event | category | flops | bytes accessed | tf_op | source)
XLA Modules:
  0.0 90.2 jit_solution(8743803307580007618)
XLA Ops:
  0.7 0.0 copy-start
  0.7 87.0 %shard_map.91 = f32[5,2,272,128]{3,2,1,0:T(8,128)} custom-call(f32[5,2,272,128]{3,2,1,0:T(8,128)} %bitcast.25, s32[2,272,128]{2,1,0:T(8,128)} %bitcast.26, f32[2,272,128]{2,1,0:T(8,128)} %bitcast.27, s32[1,512]{1,0:T(1,128)} %bitcast.31, s32[4,512]{1,0:T(4,128)} %bitcast.29, f32[4,512]{1,0:T(4,128)} %bitcast.30, f32[5,512]{1,0:T(8,128)} %bitcast.28, ...), custom_call_target="tpu_custom_call" | custom-call | tf_op jit(solution)/shard_map/pallas_call | solution.py:457
  87.7 0.0 copy-done
  87.7 2.6 %bitcast_add_fusion = f32[5,16,4352]{2,1,0:T(8,128)} fusion(f32[5,16,4352]{2,1,0:T(8,128)S(1)} %copy-done, f32[5,2,272,128]{3,2,1,0:T(8,128)} %shard_map.91), kind=kLoop, calls=%fused_computation | loop fusion | flops 348160 | bytes 4177920 | tf_op jit(solution)/shard_map/add | solution.py:502
Async XLA Ops:
  0.7 87.0 %copy-start = (f32[5,16,4352]{2,1,0:T(8,128)S(1)}, f32[5,16,4352]{2,1,0:T(8,128)}, u32[]{:S(2)}) copy-start(f32[5,16,4352]{2,1,0:T(8,128)} %param.9) | copy-start | bytes 4177924

commit v4 on v3

--- a/solution.py
+++ b/solution.py
@@ -34,11 +34,17 @@
 
     barrier = pltpu.get_barrier_semaphore()
 
-    def greet(i, carry):
-        pl.semaphore_signal(barrier, inc=1, device_id={"tile": lax.rem(tile + i, tiles)})
-        return carry
-
-    lax.fori_loop(1, tiles, greet, 0)
+    def each_other(act):
+        group = next(g for g in (7, 5, 3, 1) if (tiles - 1) % g == 0)
+
+        def some(i, carry):
+            for k in range(1, group + 1):
+                act(lax.rem(tile + i * group + k, tiles))
+            return carry
+
+        lax.fori_loop(0, (tiles - 1) // group, some, 0)
+
+    each_other(lambda t: pl.semaphore_signal(barrier, inc=1, device_id={"tile": t}))
     for i in range(1, levs):
         pl.semaphore_signal(barrier, inc=1, device_id={"lev": lax.rem(lev + i, levs)})
 
@@ -158,20 +164,16 @@
         left = left - piece.astype(F32)
     sbuf[...] = message.reshape(SRC, 1, 256)
 
-    def profile_copy(to, frm):
+    def profile_copy(src, dst, to):
         return pltpu.make_async_remote_copy(
-            src_ref=sbuf.at[to], dst_ref=rbuf.at[tile], send_sem=prof_send.at[to], recv_sem=prof_recv.at[frm],
-            device_id={"tile": to},
+            src_ref=src, dst_ref=dst, send_sem=prof_send.at[0], recv_sem=prof_recv.at[0], device_id={"tile": to}
         )
 
-    def send_profiles(i, carry):
-        to = lax.rem(tile + i, tiles)
-        profile_copy(to, tile).start()
-        return carry
-
-    lax.fori_loop(1, tiles, send_profiles, 0)
-    own = pltpu.make_async_copy(sbuf.at[tile], rbuf.at[tile], prof_recv.at[tile])
+    each_other(lambda t: profile_copy(sbuf.at[t], rbuf.at[tile], t).start())
+    own = pltpu.make_async_copy(sbuf.at[tile], rbuf.at[tile], prof_recv.at[1])
     own.start()
+    others = pl.ds(0, tiles - 1)
+    every = profile_copy(sbuf.at[others], rbuf.at[others], lax.rem(tile + 1, tiles))
 
     def coefficients(lo, hi):
         def one(r, carry):
@@ -259,12 +261,7 @@
     coefficients(DEPTH + 1, DEPTH + height - 1)
     inner(u0)
 
-    def got_profile(i, carry):
-        frm = lax.rem(tile + i, tiles)
-        profile_copy(frm, frm).wait_recv()
-        return carry
-
-    lax.fori_loop(1, tiles, got_profile, 0)
+    every.wait_recv()
     own.wait()
     heard = jnp.concatenate([rbuf[...].reshape(SRC, 256), jnp.zeros((128 - SRC, 256), F32)], axis=0)
     turned = jnp.transpose(heard)
@@ -419,11 +416,7 @@
             at = front + pitch * l
             out[l, part, here, :] = rh[r, 0:n_t, :] * u2[DEPTH + r, at:at + n_t, :]
 
-    def sent_profile(i, carry):
-        profile_copy(lax.rem(tile + i, tiles), tile).wait_send()
-        return carry
-
-    lax.fori_loop(1, tiles, sent_profile, 0)
+    every.wait_send()
     for i in range(1, levs):
         level_copy(i).wait_send()
 
@@ -480,8 +473,8 @@
             pltpu.VMEM((levs, 8, slots), F32),
             pltpu.SemaphoreType.DMA((3, 2, DEPTH // CHUNK)),
             pltpu.SemaphoreType.DMA((3, 2, DEPTH // CHUNK)),
-            pltpu.SemaphoreType.DMA((SRC,)),
-            pltpu.SemaphoreType.DMA((SRC,)),
+            pltpu.SemaphoreType.DMA((2,)),
+            pltpu.SemaphoreType.DMA((2,)),
             pltpu.SemaphoreType.DMA((levs,)),
             pltpu.SemaphoreType.DMA((levs,)),
         ],

time: 90.4 us -> 88.2 us (0.976)
  Pallas kernels: 87 us -> 84.8 us
    pallas_call x1, Pallas kernels: 87 us -> 84.8 us  [per_device(): pl.pallas_call(functools.partial(kernel, dims), out_shape=jax.ShapeDtypeS...]
where the time goes in v4:
time: 88.2 us; the launch traced here: 88 us
  Pallas kernels  84.8 us (96%)
  other arithmetic  2.57 us (3%)
    pallas_call x1, Pallas kernels, per_device(): pl.pallas_call(functools.partial(kernel, dims), out_shape=jax.ShapeDtypeS...  84.8 us
    add x1, other arithmetic, per_device(): return control + untiled(returned, height, n_t)  2.57 us

profile of v4, /device:TPU:1, one launch (start us, length us, event | category | flops | bytes accessed | tf_op | source)
XLA Modules:
  0.0 88.0 jit_solution(13337177125409179221)
XLA Ops:
  0.7 0.0 copy-start
  0.7 84.8 %shard_map.91 = f32[5,2,272,128]{3,2,1,0:T(8,128)} custom-call(f32[5,2,272,128]{3,2,1,0:T(8,128)} %bitcast.25, s32[2,272,128]{2,1,0:T(8,128)} %bitcast.26, f32[2,272,128]{2,1,0:T(8,128)} %bitcast.27, s32[1,512]{1,0:T(1,128)} %bitcast.31, s32[4,512]{1,0:T(4,128)} %bitcast.29, f32[4,512]{1,0:T(4,128)} %bitcast.30, f32[5,512]{1,0:T(8,128)} %bitcast.28, ...), custom_call_target="tpu_custom_call" | custom-call | tf_op jit(solution)/shard_map/pallas_call | solution.py:450
  85.5 0.0 copy-done
  85.5 2.6 %bitcast_add_fusion = f32[5,16,4352]{2,1,0:T(8,128)} fusion(f32[5,16,4352]{2,1,0:T(8,128)S(1)} %copy-done, f32[5,2,272,128]{3,2,1,0:T(8,128)} %shard_map.91), kind=kLoop, calls=%fused_computation | loop fusion | flops 348160 | bytes 4177920 | tf_op jit(solution)/shard_map/add | solution.py:495
Async XLA Ops:
  0.7 84.8 %copy-start = (f32[5,16,4352]{2,1,0:T(8,128)S(1)}, f32[5,16,4352]{2,1,0:T(8,128)}, u32[]{:S(2)}) copy-start(f32[5,16,4352]{2,1,0:T(8,128)} %param.9) | copy-start | bytes 4177924

commit v5 on v4

--- a/solution.py
+++ b/solution.py
@@ -261,6 +261,29 @@
     coefficients(DEPTH + 1, DEPTH + height - 1)
     inner(u0)
 
+    def more_roots(chunk):
+        wait_halo(0, chunk, root=True)
+        coefficients(DEPTH - CHUNK * chunk - 1, DEPTH - CHUNK * chunk + 1)
+        coefficients(DEPTH + height + CHUNK * chunk - 1, DEPTH + height + CHUNK * chunk + 1)
+        wait_halo(0, chunk)
+
+    more_roots(0)
+    nearest(u0)
+
+    def arrived(chunk, carry):
+        more_roots(chunk)
+        farther(u0, chunk)
+        return carry
+
+    lax.fori_loop(1, chunks, arrived, 0)
+
+    def all_sent(chunk, carry):
+        wait_sent(0, chunk, root=True)
+        wait_sent(0, chunk)
+        return carry
+
+    lax.fori_loop(0, chunks, all_sent, 0)
+
     every.wait_recv()
     own.wait()
     heard = jnp.concatenate([rbuf[...].reshape(SRC, 256), jnp.zeros((128 - SRC, 256), F32)], axis=0)
@@ -283,29 +306,6 @@
         return carry
 
     lax.fori_loop(0, qp // 128, one_hots, 0)
-
-    def more_roots(chunk):
-        wait_halo(0, chunk, root=True)
-        coefficients(DEPTH - CHUNK * chunk - 1, DEPTH - CHUNK * chunk + 1)
-        coefficients(DEPTH + height + CHUNK * chunk - 1, DEPTH + height + CHUNK * chunk + 1)
-        wait_halo(0, chunk)
-
-    more_roots(0)
-    nearest(u0)
-
-    def arrived(chunk, carry):
-        more_roots(chunk)
-        farther(u0, chunk)
-        return carry
-
-    lax.fori_loop(1, chunks, arrived, 0)
-
-    def all_sent(chunk, carry):
-        wait_sent(0, chunk, root=True)
-        wait_sent(0, chunk)
-        return carry
-
-    lax.fori_loop(0, chunks, all_sent, 0)
 
     for l in range(n_l):
         at = front + pitch * l

time: 88.2 us -> 78.3 us (0.89)
  Pallas kernels: 84.8 us -> 74.9 us
    pallas_call x1, Pallas kernels: 84.8 us -> 74.9 us  [per_device(): pl.pallas_call(functools.partial(kernel, dims), out_shape=jax.ShapeDtypeS...]
where the time goes in v5:
time: 78.3 us; the launch traced here: 78.2 us
  Pallas kernels  74.9 us (96%)
  other arithmetic  2.57 us (3%)
    pallas_call x1, Pallas kernels, per_device(): pl.pallas_call(functools.partial(kernel, dims), out_shape=jax.ShapeDtypeS...  74.9 us
    add x1, other arithmetic, per_device(): return control + untiled(returned, height, n_t)  2.57 us

profile of v5, /device:TPU:1, one launch (start us, length us, event | category | flops | bytes accessed | tf_op | source)
XLA Modules:
  0.0 78.2 jit_solution(3840789231012313085)
XLA Ops:
  0.7 0.0 copy-start
  0.7 74.9 %shard_map.91 = f32[5,2,272,128]{3,2,1,0:T(8,128)} custom-call(f32[5,2,272,128]{3,2,1,0:T(8,128)} %bitcast.25, s32[2,272,128]{2,1,0:T(8,128)} %bitcast.26, f32[2,272,128]{2,1,0:T(8,128)} %bitcast.27, s32[1,512]{1,0:T(1,128)} %bitcast.31, s32[4,512]{1,0:T(4,128)} %bitcast.29, f32[4,512]{1,0:T(4,128)} %bitcast.30, f32[5,512]{1,0:T(8,128)} %bitcast.28, ...), custom_call_target="tpu_custom_call" | custom-call | tf_op jit(solution)/shard_map/pallas_call | solution.py:450
  75.6 0.0 copy-done
  75.6 2.6 %bitcast_add_fusion = f32[5,16,4352]{2,1,0:T(8,128)} fusion(f32[5,16,4352]{2,1,0:T(8,128)S(1)} %copy-done, f32[5,2,272,128]{3,2,1,0:T(8,128)} %shard_map.91), kind=kLoop, calls=%fused_computation | loop fusion | flops 348160 | bytes 4177920 | tf_op jit(solution)/shard_map/add | solution.py:495
Async XLA Ops:
  0.7 74.9 %copy-start = (f32[5,16,4352]{2,1,0:T(8,128)S(1)}, f32[5,16,4352]{2,1,0:T(8,128)}, u32[]{:S(2)}) copy-start(f32[5,16,4352]{2,1,0:T(8,128)} %param.9) | copy-start | bytes 4177924
